TPU v7x, 128 devices: a whole 4x4x4 slice. The times are simulated.
128 devices in a mesh: row: 8 (over x, core), col: 16 (over z, y).
Axes of the slice: x: 4, y: 4, z: 4, core: 2. Of those that a mesh axis runs over, the one named last changes fastest.
Arguments:
- embeddings: float32 [49152, 128], P(('row', 'col')), may hold values from -17 to 17
- counts: int32 [32, 49152], P(None, ('row', 'col')), may hold values from 0 to 20, as said below
- raw_weights: float32 [32], replicated, may hold values from 0.25 to 4
Outputs:
- center: float32 [49152], P(('row', 'col'))
- scale_u: float32 [32, 49152], P(None, ('row', 'col'))
- scale_v: float32 [32, 49152], P(None, ('row', 'col'))
- misfit: float32 [32], replicated
Inputs may be any that keep to these rules, and one draw needn't show every extreme that they name: non-negative cell counts; every time point has at least one cell.
All inputs are finite; a program needn't handle non-finite values.
Results may differ from a plain program's by a relative error of at most 0.0021.
The roundings to bfloat16 on the way count: a program that leaves them out, or rounds other values in their place, can miss the bound.
Values may be sent and summed in bfloat16 or wider, within the bound.
A program may use at most 128 MiB of HBM per device.

v0:
```python
import functools

import jax
import jax.numpy as jnp
from jax import lax
from jax.experimental import pallas as pl
from jax.experimental.pallas import tpu as pltpu
from jax.sharding import PartitionSpec as P

GROUP_I = ((0, 0), (1, 0), (3, 0), (0, 1), (3, 1), (2, 0), (1, 1), (2, 1))
GROUP_J = ((0, 0), (0, 1), (3, 0), (1, 0), (3, 1), (2, 0), (1, 1), (2, 1))
MESH = pl.DeviceIdType.MESH
SLOPE = 14.426950408889634
HIST = 32
OWN = 384
PER_I, PER_J = 16, 8
ROWS, COLS = OWN * PER_I, OWN * PER_J
BUILD_I, BUILD_J = 1536, 768
PASS_J = 768
EARLY = 3
FORWARDED = (1, 2, 3, 4, 5, 6)
ORDER = (1, 2, 3, 4, 5, 15, 14, 13, 12, 11, 10, 9, 8, 7, 6)


def body(
    total_pts,
    emb_hbm,
    counts_hbm,
    weights_hbm,
    center_hbm,
    scale_u_hbm,
    scale_v_hbm,
    misfit_hbm,
    tile,
    unit_i,
    unit_j,
    x_buf,
    y_part,
    y_send,
    y_recv,
    first_part,
    first_row,
    first_recv,
    target,
    v_first,
    emb_ref,
    counts_ref,
    weights_ref,
    counts_all,
    row_all,
    wide_i,
    wide_j,
    moved_j,
    mass_i,
    raw_j,
    center_ref,
    scale_u_ref,
    scale_v_ref,
    misfit_ref,
    load_sem,
    store_sem,
    ready,
    send_unit_i,
    recv_unit_i,
    send_unit_j,
    recv_unit_j,
    send_counts,
    recv_counts,
    send_first,
    recv_first,
    send_x,
    recv_x,
    send_y,
    recv_y,
    send_wide_i,
    recv_wide_i,
    send_wide_j,
    recv_wide_j,
    send_mass_i,
    recv_mass_i,
    send_raw_j,
    recv_raw_j,
    send_moved_j,
    recv_moved_j,
):
    row, col = lax.axis_index("row"), lax.axis_index("col")
    x, core = lax.div(row, 2), lax.rem(row, 2)
    z, y = lax.div(col, 4), lax.rem(col, 4)

    def device(nx, ncore, nz, ny):
        return (nx * 2 + ncore, nz * 4 + ny)

    def device_i(k):
        dx, pair = GROUP_I[k // 2]
        ncore = 1 - core if k % 2 else core
        return device(lax.rem(x + 4 - dx, 4), ncore, z, y + 1 - 2 * lax.rem(y, 2) if pair else y)

    def device_j(k):
        dz, pair = GROUP_J[k]
        return device(x, core, lax.rem(z + 4 - dz, 4), 3 - y if pair else y)

    def owner_j(k):
        dz, pair = GROUP_J[k]
        return device(x, core, lax.rem(z + dz, 4), 3 - y if pair else y)

    sibling = device(x, 1 - core, z, y)
    near = [sibling] + [device_i(2 * s) for s in (1, 2, 3)] + [device_j(s) for s in (1, 2, 3)]

    def remote(device_id, src, dst, send, recv):
        return pltpu.make_async_remote_copy(
            src_ref=src, dst_ref=dst, send_sem=send, recv_sem=recv,
            device_id=device_id, device_id_type=MESH,
        )

    def start(copies):
        for copy in copies:
            copy.start()

    def received(copies):
        for copy in copies:
            copy.wait_recv()

    def sent(copies):
        for copy in copies:
            copy.wait_send()

    def tell_near(semaphore):
        for neighbour in near:
            pl.semaphore_signal(semaphore, inc=1, device_id=neighbour, device_id_type=MESH)

    def rows_of(k):
        return pl.ds(k * OWN, OWN)

    def lanes(value):
        return value[:, 0:128] + value[:, 128:256] + value[:, 256:384]

    loads = [
        pltpu.make_async_copy(src, dst, load_sem.at[n])
        for n, (src, dst) in enumerate(((emb_hbm, emb_ref), (counts_hbm, counts_ref), (weights_hbm, weights_ref)))
    ]
    for load in loads:
        load.start()
    barrier = pltpu.get_barrier_semaphore()
    tell_near(barrier)
    loads[0].wait()

    emb = emb_ref[...]
    squares = jnp.sum(emb * emb, axis=1, keepdims=True)
    unit = (emb * lax.rsqrt(squares + 1e-6)).astype(jnp.bfloat16)
    unit_i[0:OWN, :] = unit
    unit_j[0:OWN, :] = unit

    unit_copies_i = {
        k: remote(
            device_i(k), unit_i.at[rows_of(0)], unit_i.at[rows_of(k)],
            send_unit_i.at[k], recv_unit_i.at[k],
        )
        for k in (1, 2, 4, 6, 8, 10, 12, 14)
    }
    unit_copies_j = {
        k: remote(
            device_j(k), unit_j.at[rows_of(0)], unit_j.at[rows_of(k)],
            send_unit_j.at[k], recv_unit_j.at[k],
        )
        for k in range(1, PER_J)
    }
    forwards = {
        s: remote(
            sibling, unit_i.at[rows_of(2 * s)], unit_i.at[rows_of(2 * s + 1)],
            send_unit_i.at[2 * s + 1], recv_unit_i.at[2 * s + 1],
        )
        for s in range(1, 8)
    }

    def send_units(slots):
        for s in slots:
            unit_copies_i[2 * s].start()
            unit_copies_j[s].start()

    pl.semaphore_wait(barrier, len(near))
    unit_copies_i[1].start()
    send_units((1, 2, 3))
    for hops in range(2):
        tell_near(ready.at[hops])
        pl.semaphore_wait(ready.at[hops], len(near))
    sent([unit_copies_i[k] for k in (2, 4, 6)])
    sent([unit_copies_j[k] for k in (1, 2, 3)])
    send_units((7, 4, 5, 6))

    def exchange_j(buf, index, send, recv):
        return [
            remote(
                device_j(k), buf.at[index, 0], buf.at[index, k],
                send.at[index, k], recv.at[index, k],
            )
            for k in range(PER_J - 1, 0, -1)
        ]

    def exchange_i(buf, index, send, recv):
        return [
            remote(
                device_i(k), buf.at[index, 0], buf.at[index, k],
                send.at[index, k], recv.at[index, k],
            )
            for k in range(PER_I - 1, 0, -1)
        ]

    def share(buf, forwarded, send, recv):
        direct = {
            k: remote(
                device_i(k), buf.at[:, rows_of(0)], buf.at[:, rows_of(k)], send.at[k], recv.at[k]
            )
            for k in range(1, PER_I)
            if k % 2 == 0 or k // 2 not in forwarded
        }
        passed_on = {
            s: remote(
                sibling, buf.at[:, rows_of(2 * s)], buf.at[:, rows_of(2 * s + 1)],
                send.at[2 * s + 1], recv.at[2 * s + 1],
            )
            for s in forwarded
        }
        return direct, passed_on

    loads[1].wait()
    loads[2].wait()
    counts = counts_ref[...].astype(jnp.float32)
    raw_weights = weights_ref[...]
    eye = lax.broadcasted_iota(jnp.int32, (HIST, HIST), 0) == lax.broadcasted_iota(
        jnp.int32, (HIST, HIST), 1
    )
    weights = jnp.sum(
        jnp.where(eye, raw_weights / jnp.sum(raw_weights), 0.0), axis=1, keepdims=True
    )
    totals_j = exchange_j(wide_j, 0, send_wide_j, recv_wide_j)
    totals_i = exchange_i(wide_i, 0, send_wide_i, recv_wide_i)
    wide_j[0, 0] = lanes(counts)
    start(totals_j)
    first_part[...] = jnp.zeros_like(first_part)
    first_copies = {
        k: remote(
            owner_j(k), first_row.at[:, rows_of(k)], first_recv.at[k],
            send_first.at[k], recv_first.at[k],
        )
        for k in range(1, PER_J)
    }

    counts_all[:, 0:OWN] = counts.astype(jnp.bfloat16)
    counts_copies, counts_forwards = share(counts_all, tuple(range(1, 8)), send_counts, recv_counts)

    def forward(slots):
        for s in slots:
            unit_copies_i[2 * s].wait_recv()
            forwards[s].start()

    def columns_arrived(slots):
        for s in slots:
            unit_copies_j[s].wait_recv()

    def rows_arrived(slots):
        for s in slots:
            forwards[s].wait_recv()

    def build_block(at_i, at_j):
        gram = lax.dot_general(
            unit_i[at_i, :], unit_j[at_j, :], (((1,), (1,)), ((), ())),
            preferred_element_type=jnp.float32,
        )
        value = jnp.exp2(gram * SLOPE - SLOPE)
        tile[at_i, at_j] = value.astype(jnp.bfloat16)
        first_part[:, at_j] += jnp.sum(
            value.reshape(at_i.size // 8, 8, at_j.size), axis=0
        )

    def build(n, carry):
        t = (n >= 1).astype(jnp.int32) + (n >= 4).astype(jnp.int32) + (n >= 9).astype(jnp.int32)
        m = n - t * t
        down = (m < t).astype(jnp.int32)
        i = down * m + (1 - down) * t
        j = down * t + (1 - down) * (2 * t - m)

        @pl.when(n == 0)
        def _():
            forward((1,))
            unit_copies_i[1].wait_recv()
            columns_arrived((1,))
            forward((2, 3))
            rows_arrived((1,))

        @pl.when(n == 1)
        def _():
            columns_arrived((2, 3))

        @pl.when(n == 2)
        def _():
            rows_arrived((2, 3))

        @pl.when(n == 4)
        def _():
            columns_arrived((4, 5))
            forward((4, 5))

        @pl.when(n == 6)
        def _():
            rows_arrived((4, 5))
            received(totals_j)
            wide_i[0, 0] = jnp.sum(wide_j[0], axis=0)
            start(totals_i)

        build_block(
            pl.ds(pl.multiple_of(i * BUILD_I, BUILD_I), BUILD_I),
            pl.ds(pl.multiple_of(j * BUILD_J, BUILD_J), BUILD_J),
        )
        return carry

    lax.fori_loop(0, 9, build, 0)
    columns_arrived((6, 7))
    forward((6, 7))
    start(counts_copies.values())
    build_block(pl.ds(0, 3 * BUILD_I), pl.ds(3 * BUILD_J, BUILD_J))
    rows_arrived((6, 7))
    for last in (1, 0):
        build_block(pl.ds(3 * BUILD_I, BUILD_I), pl.ds(last * 2 * BUILD_J, 2 * BUILD_J))
        done = pl.ds(last * 2 * BUILD_J, 2 * BUILD_J)
        first_row[:, done] = jnp.sum(first_part[:, done], axis=0, keepdims=True)
        start(first_copies[k] for k in range(4 * last + 3, 4 * last - 1, -1) if k)
    for s in range(1, 8):
        counts_copies[2 * s].wait_recv()
        counts_forwards[s].start()

    first_recv[0] = first_row[:, 0:OWN]
    sent([unit_copies_i[k] for k in (1, 8, 10, 12, 14)])
    sent([unit_copies_j[k] for k in (4, 5, 6, 7)])
    sent(forwards.values())
    sent(counts_copies.values())
    sent(counts_forwards.values())
    sent(totals_j)
    received(totals_i)
    totals = jnp.sum(jnp.sum(wide_i[0], axis=0), axis=1, keepdims=True)
    per_count = total_pts / totals
    target[...] = counts * per_count
    counts_copies[1].wait_recv()
    received(counts_forwards.values())
    received(first_copies.values())
    row_sum = jnp.sum(first_recv[...], axis=0)

    stores = [
        pltpu.make_async_copy(src, dst, store_sem.at[n])
        for n, (src, dst) in enumerate(
            (
                (center_ref, center_hbm),
                (scale_u_ref, scale_u_hbm),
                (scale_v_ref, scale_v_hbm),
                (misfit_ref, misfit_hbm),
            )
        )
    ]

    def gather_value(index, value):
        x_buf[index, :, 0:OWN] = value.astype(jnp.bfloat16)
        direct, passed_on = share(x_buf.at[index], FORWARDED, send_x.at[index], recv_x.at[index])
        start(direct[k] for k in ORDER if k in direct)

        def pass_on(slots):
            for s in slots:
                if s in passed_on:
                    direct[2 * s].wait_recv()
                    passed_on[s].start()

        def arrive(first, last):
            if first == 1:
                pass_on((1, 2, 3))
            if first == 2:
                pass_on((4, 5, 6))
            if first == EARLY:
                pass_on((7,))
            for s in range(first, last):
                if s in passed_on:
                    passed_on[s].wait_recv()
                else:
                    received(direct[k] for k in (2 * s, 2 * s + 1) if k)

        def leave():
            sent(direct.values())
            sent(passed_on.values())

        return arrive, leave

    def gather_first(row_sum):
        row_all[:, 0:OWN] = row_sum
        copies = {
            k: remote(
                device_i(k), row_all.at[:, rows_of(0)], row_all.at[:, rows_of(k)],
                send_x.at[0, k], recv_x.at[0, k],
            )
            for k in range(1, PER_I)
        }
        start(copies[k] for k in ORDER)

        def arrive(first, last):
            received(copies[k] for k in range(2 * first, 2 * last) if k)
            at = pl.ds(first * 2 * OWN, (last - first) * 2 * OWN)
            x_buf[0, :, at] = (
                counts_all[:, at].astype(jnp.float32) * per_count / row_all[:, at]
            ).astype(jnp.bfloat16)

        return arrive, lambda: sent(copies.values())

    def run_pass(index, gather, before, between):
        arrive, leave = gather
        copies = {
            k: remote(
                owner_j(k), y_send.at[index, :, rows_of(k)], y_recv.at[index, k],
                send_y.at[index, k], recv_y.at[index, k],
            )
            for k in range(1, PER_J)
        }
        y_part[...] = jnp.zeros_like(y_part)
        before()

        def by_rows(s, carry):
            for which in range(EARLY):

                @pl.when(s == which)
                def _():
                    arrive(which, which + 1)

            at = pl.ds(pl.multiple_of(s * 2 * OWN, 2 * OWN), 2 * OWN)
            y_part[...] += jnp.dot(
                x_buf[index, :, at], tile[at, :], preferred_element_type=jnp.float32
            )
            return carry

        lax.fori_loop(0, EARLY, by_rows, 0)
        between()
        arrive(EARLY, 8)
        late = pl.ds(EARLY * 2 * OWN, ROWS - EARLY * 2 * OWN)

        def by_columns(n, carry):
            q = 3 - n
            at = pl.ds(pl.multiple_of(q * PASS_J, PASS_J), PASS_J)
            value = y_part[:, at] + jnp.dot(
                x_buf[index, :, late], tile[late, at], preferred_element_type=jnp.float32
            )
            y_part[:, at] = value
            y_send[index, :, at] = value.astype(jnp.bfloat16)
            for which in range(4):

                @pl.when(q == which)
                def _():
                    for k in (2 * which + 1, 2 * which):
                        if k:
                            copies[k].start()

            return carry

        lax.fori_loop(0, 4, by_columns, 0)
        leave()
        received(copies.values())
        total = y_part[:, 0:OWN]
        for k in range(1, PER_J):
            total += y_recv[index, k].astype(jnp.float32)
        return total, lambda: sent(copies.values())

    def raw(col_sum):
        return jnp.exp(jnp.sum(weights * jnp.log(col_sum), axis=0, keepdims=True))

    def scalar(value):
        return jnp.sum(value, axis=1, keepdims=True)

    def nothing():
        return None

    def first_sent():
        sent(first_copies.values())
        sent(totals_i)

    col_sum, y_sent = run_pass(0, gather_first(row_sum), first_sent, nothing)
    raw_center = raw(col_sum)
    v_first[...] = raw_center / col_sum
    mass_copies_j = exchange_j(raw_j, 0, send_raw_j, recv_raw_j)
    mass_copies_i = exchange_i(mass_i, 0, send_mass_i, recv_mass_i)

    def mass_begin():
        raw_j[0, 0] = raw_center
        start(mass_copies_j)
        y_sent()

    def mass_next():
        received(mass_copies_j)
        mass_i[0, 0] = lanes(jnp.sum(raw_j[0], axis=0))
        start(mass_copies_i)
        sent(mass_copies_j)

    row_sum, y_sent = run_pass(1, gather_value(1, v_first[...]), mass_begin, mass_next)
    received(mass_copies_i)
    factor = total_pts / scalar(jnp.sum(mass_i[0], axis=0))
    scale_u = target[...] / (row_sum * factor)
    scale_v = v_first[...] * factor

    def second_sent():
        scale_u_ref[...] = scale_u
        stores[1].start()
        sent(mass_copies_i)
        y_sent()

    col_sum, y_sent = run_pass(2, gather_value(2, scale_u), second_sent, nothing)
    raw_center = raw(col_sum)
    raw_j[1, 0] = raw_center
    mass_copies_j = exchange_j(raw_j, 1, send_raw_j, recv_raw_j)
    start(mass_copies_j)
    mass_copies_i = exchange_i(mass_i, 1, send_mass_i, recv_mass_i)
    error_copies_j = exchange_j(moved_j, 0, send_moved_j, recv_moved_j)
    error_copies_i = exchange_i(mass_i, 2, send_mass_i, recv_mass_i)
    moved_j[0, 0] = scale_v * col_sum
    start(error_copies_j)
    y_sent()
    received(mass_copies_j)
    mass_i[1, 0] = lanes(jnp.sum(raw_j[1], axis=0))
    start(mass_copies_i)
    sent(mass_copies_j)
    received(error_copies_j)
    sent(error_copies_j)
    received(mass_copies_i)
    factor = total_pts / scalar(jnp.sum(mass_i[1], axis=0))
    error = jnp.zeros((HIST, OWN), jnp.float32)
    for k in range(PER_J):
        error += jnp.abs(moved_j[0, k] - raw_j[1, k] * factor)
    error = jnp.sum(lanes(error), axis=1, keepdims=True) / total_pts
    wide_eye = lax.broadcasted_iota(jnp.int32, (HIST, 128), 0) == lax.broadcasted_iota(
        jnp.int32, (HIST, 128), 1
    )
    mass_i[2, 0] = jnp.sum(jnp.where(wide_eye, error, 0.0), axis=0, keepdims=True)
    start(error_copies_i)
    center = raw_center * factor
    center_ref[...] = center
    scale_v_ref[...] = center / col_sum
    stores[0].start()
    stores[2].start()
    sent(mass_copies_i)
    received(error_copies_i)
    misfit_ref[...] = jnp.sum(mass_i[2], axis=0)[:, 0:HIST]
    stores[3].start()
    sent(error_copies_i)
    for store in stores:
        store.wait()


def hand_over(center, scale_u, scale_v, misfit, center_out, scale_u_out, scale_v_out, misfit_out):
    center_out[...] = center[0]
    scale_u_out[...] = scale_u[...]
    scale_v_out[...] = scale_v[...]
    misfit_out[...] = misfit[0]


def shards(embeddings, counts, raw_weights):
    total_pts = embeddings.shape[0] * lax.axis_size("row") * lax.axis_size("col")
    vmem = pl.BlockSpec(memory_space=pltpu.VMEM)
    anywhere = pl.BlockSpec(memory_space=pl.ANY)
    f32, bf16, dma = jnp.float32, jnp.bfloat16, pltpu.SemaphoreType.DMA
    pair_i, pair_j = [dma((PER_I,))] * 2, [dma((PER_J,))] * 2
    center, scale_u, scale_v, misfit = pl.pallas_call(
        functools.partial(body, total_pts),
        out_shape=(
            jax.ShapeDtypeStruct((1, OWN), f32),
            jax.ShapeDtypeStruct((HIST, OWN), f32),
            jax.ShapeDtypeStruct((HIST, OWN), f32),
            jax.ShapeDtypeStruct((1, HIST), f32),
        ),
        in_specs=[anywhere] * 3,
        out_specs=(anywhere,) * 4,
        scratch_shapes=[
            pltpu.VMEM((ROWS, COLS), bf16),
            pltpu.VMEM((ROWS, 128), bf16),
            pltpu.VMEM((COLS, 128), bf16),
            pltpu.VMEM((3, HIST, ROWS), bf16),
            pltpu.VMEM((HIST, COLS), f32),
            pltpu.VMEM((3, HIST, COLS), bf16),
            pltpu.VMEM((3, PER_J, HIST, OWN), bf16),
            pltpu.VMEM((8, COLS), f32),
            pltpu.VMEM((1, COLS), f32),
            pltpu.VMEM((PER_J, 1, OWN), f32),
            pltpu.VMEM((HIST, OWN), f32),
            pltpu.VMEM((HIST, OWN), f32),
            pltpu.VMEM((OWN, 128), f32),
            pltpu.VMEM((HIST, OWN), jnp.int32),
            pltpu.VMEM((1, HIST), f32),
            pltpu.VMEM((HIST, ROWS), bf16),
            pltpu.VMEM((1, ROWS), f32),
            pltpu.VMEM((1, PER_I, HIST, 128), f32),
            pltpu.VMEM((1, PER_J, HIST, 128), f32),
            pltpu.VMEM((1, PER_J, HIST, OWN), f32),
            pltpu.VMEM((3, PER_I, 1, 128), f32),
            pltpu.VMEM((2, PER_J, 1, OWN), f32),
            pltpu.VMEM((1, OWN), f32),
            pltpu.VMEM((HIST, OWN), f32),
            pltpu.VMEM((HIST, OWN), f32),
            pltpu.VMEM((1, HIST), f32),
            dma((3,)),
            dma((4,)),
            pltpu.SemaphoreType.REGULAR((2,)),
            *pair_i,
            *pair_j,
            *pair_i,
            *pair_j,
            *[dma((3, PER_I))] * 2,
            *[dma((3, PER_J))] * 2,
            *[dma((1, PER_I))] * 2,
            *[dma((1, PER_J))] * 2,
            *[dma((3, PER_I))] * 2,
            *[dma((2, PER_J))] * 2,
            *[dma((1, PER_J))] * 2,
        ],
        compiler_params=pltpu.CompilerParams(
            collective_id=0, has_side_effects=True, vmem_limit_bytes=62 * 1024 * 1024
        ),
    )(embeddings, counts, raw_weights.reshape(1, HIST))
    return pl.pallas_call(
        hand_over,
        out_shape=(
            jax.ShapeDtypeStruct((OWN,), f32),
            jax.ShapeDtypeStruct((HIST, OWN), f32),
            jax.ShapeDtypeStruct((HIST, OWN), f32),
            jax.ShapeDtypeStruct((HIST,), f32),
        ),
        in_specs=[vmem] * 4,
        out_specs=(vmem,) * 4,
    )(center, scale_u, scale_v, misfit)


def solution(mesh):
    placed = (P(("row", "col"), None), P(None, ("row", "col")), P())
    return jax.shard_map(
        shards,
        mesh=mesh,
        in_specs=placed,
        out_specs=(P(("row", "col")), P(None, ("row", "col")), P(None, ("row", "col")), P()),
        check_vma=False,
    )
```

profile of v0, /device:TPU:1, one launch (start us, length us, event | category | flops | bytes accessed | tf_op | source)
XLA Modules:
  0.0 94.7 jit_solution(7172605244753898033)
XLA Ops:
  0.6 92.6 %shard_map.66 = (f32[1,384]{1,0:T(1,128)}, f32[32,384]{1,0:T(8,128)}, f32[32,384]{1,0:T(8,128)}, f32[1,32]{1,0:T(1,128)}) custom-call(f32[384,128]{1,0:T(8,128)} %emb_hbm.1, s32[32,384]{1,0:T(8,128)} %counts_hbm.1, f32[1,32]{1,0:T(1,128)} %bitcast.1), custom_call_target="tpu_custom_call" | custom-call | tf_op jit(solution)/shard_map/pallas_call | solution.py:562
  93.2 1.5 %shard_map.67 = (f32[384]{0:T(512)}, f32[32,384]{1,0:T(8,128)}, f32[32,384]{1,0:T(8,128)}, f32[32]{0:T(128)}) custom-call(f32[1,384]{1,0:T(1,128)} %get-tuple-element.8.center, f32[32,384]{1,0:T(8,128)} %get-tuple-element.9.scale_u, f32[32,384]{1,0:T(8,128)} %get-tuple-element.10.scale_v, f32[1,32]{1,0:T(1,128)} %get-tuple-element.11.misfit), custom_call_target="tpu_custom_call" | custom-call | tf_op jit(solution)/shard_map/pallas_call | solution.py:618
where the time goes:
time: 94.9 us; the launch traced here: 94.7 us
  Pallas kernels  94.1 us (99%)
    pallas_call x1, Pallas kernels, shards(): pl.pallas_call(functools.partial(body, total_pts), out_shape=(jax.ShapeDt...  92.6 us

commit v1 on v0

--- a/solution.py
+++ b/solution.py
@@ -18,8 +18,22 @@
 BUILD_I, BUILD_J = 1536, 768
 PASS_J = 768
 EARLY = 3
-FORWARDED = (1, 2, 3, 4, 5, 6)
 ORDER = (1, 2, 3, 4, 5, 15, 14, 13, 12, 11, 10, 9, 8, 7, 6)
+
+
+class Together:
+    def __init__(self, copies, outgoing, incoming):
+        self.copies, self.outgoing, self.incoming = copies, outgoing, incoming
+
+    def start(self):
+        for copy in self.copies:
+            copy.start()
+
+    def wait_send(self):
+        self.outgoing.wait_send()
+
+    def wait_recv(self):
+        self.incoming.wait_recv()
 
 
 def body(
@@ -187,40 +201,28 @@
     sent([unit_copies_j[k] for k in (1, 2, 3)])
     send_units((7, 4, 5, 6))
 
+    def together(copies, left, landed, send, recv):
+        return Together(
+            copies, remote(sibling, left, left, send, recv), remote(sibling, landed, landed, send, recv)
+        )
+
     def exchange_j(buf, index, send, recv):
-        return [
-            remote(
-                device_j(k), buf.at[index, 0], buf.at[index, k],
-                send.at[index, k], recv.at[index, k],
-            )
+        copies = [
+            remote(device_j(k), buf.at[index, 0], buf.at[index, k], send.at[index], recv.at[index])
             for k in range(PER_J - 1, 0, -1)
         ]
+        others = buf.at[index, pl.ds(1, PER_J - 1)]
+        return [together(copies, others, others, send.at[index], recv.at[index])]
 
     def exchange_i(buf, index, send, recv):
-        return [
-            remote(
-                device_i(k), buf.at[index, 0], buf.at[index, k],
-                send.at[index, k], recv.at[index, k],
-            )
+        copies = [
+            remote(device_i(k), buf.at[index, 0], buf.at[index, k], send.at[index], recv.at[index])
             for k in range(PER_I - 1, 0, -1)
         ]
-
-    def share(buf, forwarded, send, recv):
-        direct = {
-            k: remote(
-                device_i(k), buf.at[:, rows_of(0)], buf.at[:, rows_of(k)], send.at[k], recv.at[k]
-            )
-            for k in range(1, PER_I)
-            if k % 2 == 0 or k // 2 not in forwarded
-        }
-        passed_on = {
-            s: remote(
-                sibling, buf.at[:, rows_of(2 * s)], buf.at[:, rows_of(2 * s + 1)],
-                send.at[2 * s + 1], recv.at[2 * s + 1],
-            )
-            for s in forwarded
-        }
-        return direct, passed_on
+        others = buf.at[index, pl.ds(1, PER_I - 1)]
+        return [together(copies, others, others, send.at[index], recv.at[index])]
+
+    other_i, other_j = pl.ds(OWN, ROWS - OWN), pl.ds(OWN, COLS - OWN)
 
     loads[1].wait()
     loads[2].wait()
@@ -240,13 +242,27 @@
     first_copies = {
         k: remote(
             owner_j(k), first_row.at[:, rows_of(k)], first_recv.at[k],
-            send_first.at[k], recv_first.at[k],
+            send_first.at[0], recv_first.at[0],
         )
         for k in range(1, PER_J)
     }
+    first_all = together(
+        [], first_row.at[:, other_j], first_recv.at[pl.ds(1, PER_J - 1)], send_first.at[0], recv_first.at[0]
+    )
 
     counts_all[:, 0:OWN] = counts.astype(jnp.bfloat16)
-    counts_copies, counts_forwards = share(counts_all, tuple(range(1, 8)), send_counts, recv_counts)
+    counts_copies = [
+        together(
+            [
+                remote(
+                    device_i(k), counts_all.at[:, rows_of(0)], counts_all.at[:, rows_of(k)],
+                    send_counts.at[0], recv_counts.at[0],
+                )
+                for k in range(PER_I - 1, 0, -1)
+            ],
+            counts_all.at[:, other_i], counts_all.at[:, other_i], send_counts.at[0], recv_counts.at[0],
+        )
+    ]
 
     def forward(slots):
         for s in slots:
@@ -316,7 +332,7 @@
     lax.fori_loop(0, 9, build, 0)
     columns_arrived((6, 7))
     forward((6, 7))
-    start(counts_copies.values())
+    start(counts_copies)
     build_block(pl.ds(0, 3 * BUILD_I), pl.ds(3 * BUILD_J, BUILD_J))
     rows_arrived((6, 7))
     for last in (1, 0):
@@ -324,24 +340,19 @@
         done = pl.ds(last * 2 * BUILD_J, 2 * BUILD_J)
         first_row[:, done] = jnp.sum(first_part[:, done], axis=0, keepdims=True)
         start(first_copies[k] for k in range(4 * last + 3, 4 * last - 1, -1) if k)
-    for s in range(1, 8):
-        counts_copies[2 * s].wait_recv()
-        counts_forwards[s].start()
 
     first_recv[0] = first_row[:, 0:OWN]
     sent([unit_copies_i[k] for k in (1, 8, 10, 12, 14)])
     sent([unit_copies_j[k] for k in (4, 5, 6, 7)])
     sent(forwards.values())
-    sent(counts_copies.values())
-    sent(counts_forwards.values())
+    sent(counts_copies)
     sent(totals_j)
     received(totals_i)
     totals = jnp.sum(jnp.sum(wide_i[0], axis=0), axis=1, keepdims=True)
     per_count = total_pts / totals
     target[...] = counts * per_count
-    counts_copies[1].wait_recv()
-    received(counts_forwards.values())
-    received(first_copies.values())
+    received(counts_copies)
+    first_all.wait_recv()
     row_sum = jnp.sum(first_recv[...], axis=0)
 
     stores = [
@@ -356,62 +367,54 @@
         )
     ]
 
-    def gather_value(index, value):
-        x_buf[index, :, 0:OWN] = value.astype(jnp.bfloat16)
-        direct, passed_on = share(x_buf.at[index], FORWARDED, send_x.at[index], recv_x.at[index])
-        start(direct[k] for k in ORDER if k in direct)
-
-        def pass_on(slots):
-            for s in slots:
-                if s in passed_on:
-                    direct[2 * s].wait_recv()
-                    passed_on[s].start()
-
-        def arrive(first, last):
-            if first == 1:
-                pass_on((1, 2, 3))
-            if first == 2:
-                pass_on((4, 5, 6))
-            if first == EARLY:
-                pass_on((7,))
-            for s in range(first, last):
-                if s in passed_on:
-                    passed_on[s].wait_recv()
-                else:
-                    received(direct[k] for k in (2 * s, 2 * s + 1) if k)
-
-        def leave():
-            sent(direct.values())
-            sent(passed_on.values())
-
-        return arrive, leave
-
-    def gather_first(row_sum):
-        row_all[:, 0:OWN] = row_sum
+    def gather(index, buf):
         copies = {
             k: remote(
-                device_i(k), row_all.at[:, rows_of(0)], row_all.at[:, rows_of(k)],
-                send_x.at[0, k], recv_x.at[0, k],
+                device_i(k), buf.at[:, rows_of(0)], buf.at[:, rows_of(k)],
+                send_x.at[index], recv_x.at[index, k // 2],
             )
             for k in range(1, PER_I)
         }
         start(copies[k] for k in ORDER)
 
+        def chip(s):
+            at = pl.ds(2 * s * OWN, 2 * OWN) if s else rows_of(1)
+            return remote(sibling, buf.at[:, at], buf.at[:, at], send_x.at[index], recv_x.at[index, s])
+
+        def leave():
+            all_sent = buf.at[:, other_i]
+            remote(sibling, all_sent, all_sent, send_x.at[index], recv_x.at[index, 0]).wait_send()
+
+        return chip, leave
+
+    def gather_value(index, value):
+        x_buf[index, :, 0:OWN] = value.astype(jnp.bfloat16)
+        chip, leave = gather(index, x_buf.at[index])
+
         def arrive(first, last):
-            received(copies[k] for k in range(2 * first, 2 * last) if k)
+            received(chip(s) for s in range(first, last))
+
+        return arrive, leave
+
+    def gather_first(row_sum):
+        row_all[:, 0:OWN] = row_sum
+        chip, leave = gather(0, row_all)
+
+        def arrive(first, last):
+            received(chip(s) for s in range(first, last))
             at = pl.ds(first * 2 * OWN, (last - first) * 2 * OWN)
             x_buf[0, :, at] = (
                 counts_all[:, at].astype(jnp.float32) * per_count / row_all[:, at]
             ).astype(jnp.bfloat16)
 
-        return arrive, lambda: sent(copies.values())
-
-    def run_pass(index, gather, before, between):
-        arrive, leave = gather
+        return arrive, leave
+
+    def run_pass(index, gathered, before, between):
+        arrive, leave = gathered
         copies = {
             k: remote(
                 owner_j(k), y_send.at[index, :, rows_of(k)], y_recv.at[index, k],
-                send_y.at[index, k], recv_y.at[index, k],
+                send_y.at[index], recv_y.at[index],
             )
             for k in range(1, PER_J)
         }
@@ -456,11 +459,15 @@
 
         lax.fori_loop(0, 4, by_columns, 0)
         leave()
-        received(copies.values())
+        y_all = together(
+            [], y_send.at[index, :, other_j], y_recv.at[index, pl.ds(1, PER_J - 1)],
+            send_y.at[index], recv_y.at[index],
+        )
+        y_all.wait_recv()
         total = y_part[:, 0:OWN]
         for k in range(1, PER_J):
             total += y_recv[index, k].astype(jnp.float32)
-        return total, lambda: sent(copies.values())
+        return total, y_all.wait_send
 
     def raw(col_sum):
         return jnp.exp(jnp.sum(weights * jnp.log(col_sum), axis=0, keepdims=True))
@@ -472,7 +479,7 @@
         return None
 
     def first_sent():
-        sent(first_copies.values())
+        first_all.wait_send()
         sent(totals_i)
 
     col_sum, y_sent = run_pass(0, gather_first(row_sum), first_sent, nothing)
@@ -601,15 +608,16 @@
             pltpu.SemaphoreType.REGULAR((2,)),
             *pair_i,
             *pair_j,
-            *pair_i,
-            *pair_j,
-            *[dma((3, PER_I))] * 2,
-            *[dma((3, PER_J))] * 2,
-            *[dma((1, PER_I))] * 2,
-            *[dma((1, PER_J))] * 2,
-            *[dma((3, PER_I))] * 2,
-            *[dma((2, PER_J))] * 2,
-            *[dma((1, PER_J))] * 2,
+            *[dma((1,))] * 2,
+            *[dma((1,))] * 2,
+            dma((3,)),
+            dma((3, PER_I // 2)),
+            *[dma((3,))] * 2,
+            *[dma((1,))] * 2,
+            *[dma((1,))] * 2,
+            *[dma((3,))] * 2,
+            *[dma((2,))] * 2,
+            *[dma((1,))] * 2,
         ],
         compiler_params=pltpu.CompilerParams(
             collective_id=0, has_side_effects=True, vmem_limit_bytes=62 * 1024 * 1024

time: 94.9 us -> 92.1 us (0.970)
  Pallas kernels: 94.1 us -> 91.3 us
    pallas_call x1, Pallas kernels: 92.6 us -> 89.8 us  [shards(): pl.pallas_call(functools.partial(body, total_pts), out_shape=(jax.ShapeDt...]
where the time goes in v1:
time: 92.1 us; the launch traced here: 91.9 us
  Pallas kernels  91.3 us (99%)
    pallas_call x1, Pallas kernels, shards(): pl.pallas_call(functools.partial(body, total_pts), out_shape=(jax.ShapeDt...  89.8 us

profile of v1, /device:TPU:1, one launch (start us, length us, event | category | flops | bytes accessed | tf_op | source)
XLA Modules:
  0.0 91.9 jit_solution(3127181133927233098)
XLA Ops:
  0.6 89.8 %shard_map.66 = (f32[1,384]{1,0:T(1,128)}, f32[32,384]{1,0:T(8,128)}, f32[32,384]{1,0:T(8,128)}, f32[1,32]{1,0:T(1,128)}) custom-call(f32[384,128]{1,0:T(8,128)} %emb_hbm.1, s32[32,384]{1,0:T(8,128)} %counts_hbm.1, f32[1,32]{1,0:T(1,128)} %bitcast.1), custom_call_target="tpu_custom_call" | custom-call | tf_op jit(solution)/shard_map/pallas_call | solution.py:569
  90.5 1.5 %shard_map.67 = (f32[384]{0:T(512)}, f32[32,384]{1,0:T(8,128)}, f32[32,384]{1,0:T(8,128)}, f32[32]{0:T(128)}) custom-call(f32[1,384]{1,0:T(1,128)} %get-tuple-element.8.center, f32[32,384]{1,0:T(8,128)} %get-tuple-element.9.scale_u, f32[32,384]{1,0:T(8,128)} %get-tuple-element.10.scale_v, f32[1,32]{1,0:T(1,128)} %get-tuple-element.11.misfit), custom_call_target="tpu_custom_call" | custom-call | tf_op jit(solution)/shard_map/pallas_call | solution.py:626

commit v2 on v1

--- a/solution.py
+++ b/solution.py
@@ -17,7 +17,7 @@
 ROWS, COLS = OWN * PER_I, OWN * PER_J
 BUILD_I, BUILD_J = 1536, 768
 PASS_J = 768
-EARLY = 3
+EARLY = 4
 ORDER = (1, 2, 3, 4, 5, 15, 14, 13, 12, 11, 10, 9, 8, 7, 6)
 
 
@@ -167,21 +167,21 @@
     unit_copies_i = {
         k: remote(
             device_i(k), unit_i.at[rows_of(0)], unit_i.at[rows_of(k)],
-            send_unit_i.at[k], recv_unit_i.at[k],
+            send_unit_i.at[0 if k < 8 else 1], recv_unit_i.at[4 if k == 1 else k // 4],
         )
         for k in (1, 2, 4, 6, 8, 10, 12, 14)
     }
     unit_copies_j = {
         k: remote(
             device_j(k), unit_j.at[rows_of(0)], unit_j.at[rows_of(k)],
-            send_unit_j.at[k], recv_unit_j.at[k],
+            send_unit_j.at[0 if k < 4 else 1], recv_unit_j.at[k // 2],
         )
         for k in range(1, PER_J)
     }
     forwards = {
         s: remote(
             sibling, unit_i.at[rows_of(2 * s)], unit_i.at[rows_of(2 * s + 1)],
-            send_unit_i.at[2 * s + 1], recv_unit_i.at[2 * s + 1],
+            send_unit_i.at[2], recv_unit_i.at[5 + s // 2],
         )
         for s in range(1, 8)
     }
@@ -190,6 +190,10 @@
         for s in slots:
             unit_copies_i[2 * s].start()
             unit_copies_j[s].start()
+
+    def units(buf, shares, semaphore):
+        some = buf.at[pl.ds(0, shares * OWN)]
+        return remote(sibling, some, some, semaphore, semaphore)
 
     pl.semaphore_wait(barrier, len(near))
     unit_copies_i[1].start()
@@ -197,8 +201,8 @@
     for hops in range(2):
         tell_near(ready.at[hops])
         pl.semaphore_wait(ready.at[hops], len(near))
-    sent([unit_copies_i[k] for k in (2, 4, 6)])
-    sent([unit_copies_j[k] for k in (1, 2, 3)])
+    units(unit_i, 4, send_unit_i.at[0]).wait_send()
+    units(unit_j, 3, send_unit_j.at[0]).wait_send()
     send_units((7, 4, 5, 6))
 
     def together(copies, left, landed, send, recv):
@@ -265,17 +269,15 @@
     ]
 
     def forward(slots):
+        units(unit_i, len(slots), recv_unit_i.at[slots[0] // 2]).wait_recv()
         for s in slots:
-            unit_copies_i[2 * s].wait_recv()
             forwards[s].start()
 
     def columns_arrived(slots):
-        for s in slots:
-            unit_copies_j[s].wait_recv()
+        units(unit_j, len(slots), recv_unit_j.at[slots[0] // 2]).wait_recv()
 
     def rows_arrived(slots):
-        for s in slots:
-            forwards[s].wait_recv()
+        units(unit_i, len(slots), recv_unit_i.at[5 + slots[0] // 2]).wait_recv()
 
     def build_block(at_i, at_j):
         gram = lax.dot_general(
@@ -342,9 +344,9 @@
         start(first_copies[k] for k in range(4 * last + 3, 4 * last - 1, -1) if k)
 
     first_recv[0] = first_row[:, 0:OWN]
-    sent([unit_copies_i[k] for k in (1, 8, 10, 12, 14)])
-    sent([unit_copies_j[k] for k in (4, 5, 6, 7)])
-    sent(forwards.values())
+    units(unit_i, 4, send_unit_i.at[1]).wait_send()
+    units(unit_j, 4, send_unit_j.at[1]).wait_send()
+    units(unit_i, 7, send_unit_i.at[2]).wait_send()
     sent(counts_copies)
     sent(totals_j)
     received(totals_i)
@@ -371,37 +373,34 @@
         copies = {
             k: remote(
                 device_i(k), buf.at[:, rows_of(0)], buf.at[:, rows_of(k)],
-                send_x.at[index], recv_x.at[index, k // 2],
+                send_x.at[index], recv_x.at[index, min(k // 2, EARLY)],
             )
             for k in range(1, PER_I)
         }
         start(copies[k] for k in ORDER)
 
-        def chip(s):
-            at = pl.ds(2 * s * OWN, 2 * OWN) if s else rows_of(1)
-            return remote(sibling, buf.at[:, at], buf.at[:, at], send_x.at[index], recv_x.at[index, s])
+        def chips(first, last):
+            at = pl.ds(max(2 * first, 1) * OWN, (2 * last - max(2 * first, 1)) * OWN)
+            remote(
+                sibling, buf.at[:, at], buf.at[:, at], send_x.at[index], recv_x.at[index, first]
+            ).wait_recv()
 
         def leave():
             all_sent = buf.at[:, other_i]
             remote(sibling, all_sent, all_sent, send_x.at[index], recv_x.at[index, 0]).wait_send()
 
-        return chip, leave
+        return chips, leave
 
     def gather_value(index, value):
         x_buf[index, :, 0:OWN] = value.astype(jnp.bfloat16)
-        chip, leave = gather(index, x_buf.at[index])
-
-        def arrive(first, last):
-            received(chip(s) for s in range(first, last))
-
-        return arrive, leave
+        return gather(index, x_buf.at[index])
 
     def gather_first(row_sum):
         row_all[:, 0:OWN] = row_sum
-        chip, leave = gather(0, row_all)
+        chips, leave = gather(0, row_all)
 
         def arrive(first, last):
-            received(chip(s) for s in range(first, last))
+            chips(first, last)
             at = pl.ds(first * 2 * OWN, (last - first) * 2 * OWN)
             x_buf[0, :, at] = (
                 counts_all[:, at].astype(jnp.float32) * per_count / row_all[:, at]
@@ -565,7 +564,6 @@
     vmem = pl.BlockSpec(memory_space=pltpu.VMEM)
     anywhere = pl.BlockSpec(memory_space=pl.ANY)
     f32, bf16, dma = jnp.float32, jnp.bfloat16, pltpu.SemaphoreType.DMA
-    pair_i, pair_j = [dma((PER_I,))] * 2, [dma((PER_J,))] * 2
     center, scale_u, scale_v, misfit = pl.pallas_call(
         functools.partial(body, total_pts),
         out_shape=(
@@ -606,12 +604,14 @@
             dma((3,)),
             dma((4,)),
             pltpu.SemaphoreType.REGULAR((2,)),
-            *pair_i,
-            *pair_j,
+            dma((3,)),
+            dma((9,)),
+            dma((2,)),
+            dma((4,)),
             *[dma((1,))] * 2,
             *[dma((1,))] * 2,
             dma((3,)),
-            dma((3, PER_I // 2)),
+            dma((3, EARLY + 1)),
             *[dma((3,))] * 2,
             *[dma((1,))] * 2,
             *[dma((1,))] * 2,

time: 92.1 us -> 91.5 us (level)
  no operation moved by 1% of the time
where the time goes in v2:
time: 91.5 us; the launch traced here: 91.3 us
  Pallas kernels  90.7 us (99%)
    pallas_call x1, Pallas kernels, shards(): pl.pallas_call(functools.partial(body, total_pts), out_shape=(jax.ShapeDt...  89.2 us

profile of v2, /device:TPU:1, one launch (start us, length us, event | category | flops | bytes accessed | tf_op | source)
XLA Modules:
  0.0 91.3 jit_solution(8923316632481621865)
XLA Ops:
  0.6 89.2 %shard_map.66 = (f32[1,384]{1,0:T(1,128)}, f32[32,384]{1,0:T(8,128)}, f32[32,384]{1,0:T(8,128)}, f32[1,32]{1,0:T(1,128)}) custom-call(f32[384,128]{1,0:T(8,128)} %emb_hbm.1, s32[32,384]{1,0:T(8,128)} %counts_hbm.1, f32[1,32]{1,0:T(1,128)} %bitcast.1), custom_call_target="tpu_custom_call" | custom-call | tf_op jit(solution)/shard_map/pallas_call | solution.py:567
  89.8 1.5 %shard_map.67 = (f32[384]{0:T(512)}, f32[32,384]{1,0:T(8,128)}, f32[32,384]{1,0:T(8,128)}, f32[32]{0:T(128)}) custom-call(f32[1,384]{1,0:T(1,128)} %get-tuple-element.8.center, f32[32,384]{1,0:T(8,128)} %get-tuple-element.9.scale_u, f32[32,384]{1,0:T(8,128)} %get-tuple-element.10.scale_v, f32[1,32]{1,0:T(1,128)} %get-tuple-element.11.misfit), custom_call_target="tpu_custom_call" | custom-call | tf_op jit(solution)/shard_map/pallas_call | solution.py:626

commit v3 on v2

--- a/solution.py
+++ b/solution.py
@@ -240,7 +240,14 @@
     )
     totals_j = exchange_j(wide_j, 0, send_wide_j, recv_wide_j)
     totals_i = exchange_i(wide_i, 0, send_wide_i, recv_wide_i)
-    wide_j[0, 0] = lanes(counts)
+    wide_eye = lax.broadcasted_iota(jnp.int32, (HIST, 128), 0) == lax.broadcasted_iota(
+        jnp.int32, (HIST, 128), 1
+    )
+
+    def as_row(value):
+        return jnp.sum(jnp.where(wide_eye, value, 0.0), axis=0, keepdims=True)
+
+    wide_j[0, 0] = as_row(jnp.sum(lanes(counts), axis=1, keepdims=True))
     start(totals_j)
     first_part[...] = jnp.zeros_like(first_part)
     first_copies = {
@@ -350,7 +357,9 @@
     sent(counts_copies)
     sent(totals_j)
     received(totals_i)
-    totals = jnp.sum(jnp.sum(wide_i[0], axis=0), axis=1, keepdims=True)
+    totals = jnp.sum(
+        jnp.where(wide_eye, jnp.sum(wide_i[0], axis=0), 0.0), axis=1, keepdims=True
+    )
     per_count = total_pts / totals
     target[...] = counts * per_count
     received(counts_copies)
@@ -533,10 +542,7 @@
     for k in range(PER_J):
         error += jnp.abs(moved_j[0, k] - raw_j[1, k] * factor)
     error = jnp.sum(lanes(error), axis=1, keepdims=True) / total_pts
-    wide_eye = lax.broadcasted_iota(jnp.int32, (HIST, 128), 0) == lax.broadcasted_iota(
-        jnp.int32, (HIST, 128), 1
-    )
-    mass_i[2, 0] = jnp.sum(jnp.where(wide_eye, error, 0.0), axis=0, keepdims=True)
+    mass_i[2, 0] = as_row(error)
     start(error_copies_i)
     center = raw_center * factor
     center_ref[...] = center
@@ -592,8 +598,8 @@
             pltpu.VMEM((1, HIST), f32),
             pltpu.VMEM((HIST, ROWS), bf16),
             pltpu.VMEM((1, ROWS), f32),
-            pltpu.VMEM((1, PER_I, HIST, 128), f32),
-            pltpu.VMEM((1, PER_J, HIST, 128), f32),
+            pltpu.VMEM((1, PER_I, 1, 128), f32),
+            pltpu.VMEM((1, PER_J, 1, 128), f32),
             pltpu.VMEM((1, PER_J, HIST, OWN), f32),
             pltpu.VMEM((3, PER_I, 1, 128), f32),
             pltpu.VMEM((2, PER_J, 1, OWN), f32),

time: 91.5 us -> 90.7 us (level)
  no operation moved by 1% of the time
where the time goes in v3:
time: 90.7 us; the launch traced here: 90.6 us
  Pallas kernels  89.9 us (99%)
    pallas_call x1, Pallas kernels, shards(): pl.pallas_call(functools.partial(body, total_pts), out_shape=(jax.ShapeDt...  88.4 us

profile of v3, /device:TPU:1, one launch (start us, length us, event | category | flops | bytes accessed | tf_op | source)
XLA Modules:
  0.0 90.6 jit_solution(13921382191639294934)
XLA Ops:
  0.6 88.4 %shard_map.66 = (f32[1,384]{1,0:T(1,128)}, f32[32,384]{1,0:T(8,128)}, f32[32,384]{1,0:T(8,128)}, f32[1,32]{1,0:T(1,128)}) custom-call(f32[384,128]{1,0:T(8,128)} %emb_hbm.1, s32[32,384]{1,0:T(8,128)} %counts_hbm.1, f32[1,32]{1,0:T(1,128)} %bitcast.1), custom_call_target="tpu_custom_call" | custom-call | tf_op jit(solution)/shard_map/pallas_call | solution.py:573
  89.1 1.5 %shard_map.67 = (f32[384]{0:T(512)}, f32[32,384]{1,0:T(8,128)}, f32[32,384]{1,0:T(8,128)}, f32[32]{0:T(128)}) custom-call(f32[1,384]{1,0:T(1,128)} %get-tuple-element.8.center, f32[32,384]{1,0:T(8,128)} %get-tuple-element.9.scale_u, f32[32,384]{1,0:T(8,128)} %get-tuple-element.10.scale_v, f32[1,32]{1,0:T(1,128)} %get-tuple-element.11.misfit), custom_call_target="tpu_custom_call" | custom-call | tf_op jit(solution)/shard_map/pallas_call | solution.py:632

commit v4 on v3

--- a/solution.py
+++ b/solution.py
@@ -18,7 +18,7 @@
 BUILD_I, BUILD_J = 1536, 768
 PASS_J = 768
 EARLY = 4
-ORDER = (1, 2, 3, 4, 5, 15, 14, 13, 12, 11, 10, 9, 8, 7, 6)
+ORDER = (1, 2, 3, 4, 5, 6, 7, 15, 14, 13, 12, 11, 10, 9, 8)
 
 
 class Together:
@@ -341,9 +341,9 @@
     lax.fori_loop(0, 9, build, 0)
     columns_arrived((6, 7))
     forward((6, 7))
-    start(counts_copies)
     build_block(pl.ds(0, 3 * BUILD_I), pl.ds(3 * BUILD_J, BUILD_J))
     rows_arrived((6, 7))
+    start(counts_copies)
     for last in (1, 0):
         build_block(pl.ds(3 * BUILD_I, BUILD_I), pl.ds(last * 2 * BUILD_J, 2 * BUILD_J))
         done = pl.ds(last * 2 * BUILD_J, 2 * BUILD_J)

time: 90.7 us -> 90.7 us (level)
  no operation moved by 1% of the time
where the time goes in v4:
time: 90.7 us; the launch traced here: 90.6 us
  Pallas kernels  89.9 us (99%)
    pallas_call x1, Pallas kernels, shards(): pl.pallas_call(functools.partial(body, total_pts), out_shape=(jax.ShapeDt...  88.4 us

profile of v4, /device:TPU:1, one launch (start us, length us, event | category | flops | bytes accessed | tf_op | source)
XLA Modules:
  0.0 90.6 jit_solution(3545584248056392190)
XLA Ops:
  0.6 88.4 %shard_map.66 = (f32[1,384]{1,0:T(1,128)}, f32[32,384]{1,0:T(8,128)}, f32[32,384]{1,0:T(8,128)}, f32[1,32]{1,0:T(1,128)}) custom-call(f32[384,128]{1,0:T(8,128)} %emb_hbm.1, s32[32,384]{1,0:T(8,128)} %counts_hbm.1, f32[1,32]{1,0:T(1,128)} %bitcast.1), custom_call_target="tpu_custom_call" | custom-call | tf_op jit(solution)/shard_map/pallas_call | solution.py:573
  89.1 1.5 %shard_map.67 = (f32[384]{0:T(512)}, f32[32,384]{1,0:T(8,128)}, f32[32,384]{1,0:T(8,128)}, f32[32]{0:T(128)}) custom-call(f32[1,384]{1,0:T(1,128)} %get-tuple-element.8.center, f32[32,384]{1,0:T(8,128)} %get-tuple-element.9.scale_u, f32[32,384]{1,0:T(8,128)} %get-tuple-element.10.scale_v, f32[1,32]{1,0:T(1,128)} %get-tuple-element.11.misfit), custom_call_target="tpu_custom_call" | custom-call | tf_op jit(solution)/shard_map/pallas_call | solution.py:632
